TPU v7x, 512 devices: a whole 4x4x16 slice. The times are simulated.
512 devices in a mesh: blk: 64 (over z_hi, y, x), grid: 8 (over z_lo, core).
Axes of the slice: x: 4, y: 4, z: 16 (z_hi: 4, z_lo: 4; z = z_hi * 4 + z_lo), core: 2. Of those that a mesh axis runs over, the one named last changes fastest.
Arguments:
- bands: float32 [128, 96, 9216], P('blk', 'grid'), may hold values from -6 to 6
Outputs:
- exchange_field: float32 [128, 96, 9216], P('blk', 'grid')
All inputs are finite; a program needn't handle non-finite values.
Results may differ from a plain program's by a relative error of at most 0.0003.
Values sent between devices are 32-bit elements; how exact they have to be, the bound alone decides.
A program may use at most 64 MiB of HBM per device.

v0:
```python
import functools

import jax
import jax.numpy as jnp
import ml_dtypes
import numpy as np
from jax import lax
from jax.experimental import pallas as pl
from jax.experimental.pallas import tpu as pltpu
from jax.sharding import PartitionSpec as P

NG = 96
BOX_EDGE = 23.47
MESH = pl.DeviceIdType.MESH
F32 = jnp.float32
BF16 = jnp.bfloat16

GRID = 8
SLAB = NG // GRID
ROWS = NG * NG // 128
SHARE = 8, 10
MSG = SHARE[1] * SLAB
FIELDS = 7

LAYER = 16
COLUMNS = (0, 1, 2, 3, 4, 7, 8, 11, 12, 13, 14, 15)
BETWEEN = LAYER - 1, 0

FORWARD = (0, 1, 2, 3, 4, 5, 6, -1, -1, -1, -1, -1, -1, -1, -1, -1)
SOLVE = (-1, -1, -1, -1, -1, -1, -1, 3, 4, 5, 6, 0, 1, 2, -1, -1)
BACKWARD = (-1, -1, -1, -1, -1, -1, -1, -1, -1, 3, 4, 5, 6, 0, 1, 2)


def hartley(rows, cols):
    angle = (rows[:, None] * cols[None, :] % NG) * (2.0 * np.pi / NG)
    return np.cos(angle) + np.sin(angle)


def split_table(table):
    parts = []
    for _ in range(3):
        part = table.astype(np.float32).astype(ml_dtypes.bfloat16)
        parts.append(part)
        table = table - part.astype(np.float64)
    return parts


def left_table(table):
    return np.concatenate([np.concatenate([part, part], axis=1) for part in split_table(table)])


def right_table(table):
    parts = [np.pad(part, ((0, 0), (0, 128 - NG))) for part in split_table(table)]
    return np.concatenate(parts, axis=1)


def tables():
    plain = np.arange(NG)
    mixed = np.arange(NG) % GRID * SLAB + np.arange(NG) // GRID
    return (
        right_table(hartley(plain, plain)),
        left_table(hartley(plain, plain)),
        left_table(hartley(plain, mixed)),
        left_table(hartley(mixed, plain)),
    )


def split(value):
    high = value.astype(BF16)
    low = (value - high.astype(F32)).astype(BF16)
    return high, low


def dot(a, b):
    return jnp.dot(a, b, preferred_element_type=F32)


def from_left(table, value):
    high, low = split(value)
    both = dot(table, jnp.concatenate([high, low], axis=0))
    return both[:NG] + (both[NG : 2 * NG] + both[2 * NG :])


def from_right(value, right_ref):
    high, low = split(value)
    above = dot(high, right_ref[:, :256])
    below = dot(low, right_ref[:, :256])
    rest = dot(high, right_ref[:, 256:])
    second = above[:, 128 : 128 + NG] + below[:, :NG]
    return above[:, :NG] + (second + (below[:, 128 : 128 + NG] + rest[:, :NG]))


def pack(plane):
    last = plane[72:96]
    return [
        jnp.concatenate([plane[24 * k : 24 * k + 24], last[:, 32 * k : 32 * k + 32]], axis=1)
        for k in range(3)
    ]


def unpack(parts):
    last = jnp.concatenate([part[:, 96:128] for part in parts], axis=1)
    return jnp.concatenate([part[:, :96] for part in parts] + [last], axis=0)


def kernel(
    blocks,
    own_ref,
    right_ref,
    plane_ref,
    there_ref,
    back_ref,
    out_ref,
    bands,
    acc,
    coulomb,
    sent,
    got,
    ret_sent,
    ret_got,
    band_out,
    band_in,
    theirs_out,
    theirs_in,
    fwd_send,
    fwd_recv,
    bwd_send,
    bwd_recv,
    self_sem,
    blk_send,
    blk_recv,
    stop,
    first_send,
    stop_recv,
    second_send,
    last_recv,
):
    blk = lax.axis_index("blk")
    me = lax.axis_index("grid")
    after = lax.rem(blk + 1, blocks)
    before = lax.rem(blk + blocks - 1, blocks)

    column = lax.rem(blk, LAYER)
    layer = blk - column
    piece = sum(jnp.where(column == c, i, 0) for i, c in enumerate(COLUMNS))
    relays = functools.reduce(jnp.logical_or, [column == c for c in COLUMNS])

    barrier = pltpu.get_barrier_semaphore()

    def greet(other):
        pl.semaphore_signal(barrier, inc=1, device_id=other, device_id_type=MESH)

    for d in range(1, GRID):
        greet((blk, lax.rem(me + d, GRID)))

    at_end = (column == 0) | (column == LAYER - 1)
    peers = GRID - 1 + jnp.where(relays, jnp.where(at_end, len(COLUMNS) + 1, 2), 0)
    for c in range(LAYER):
        linked = (column == c - 1) | (column == c + 1)
        if c in COLUMNS:
            linked = linked | ((relays if c in BETWEEN else at_end) & (column != c))
        peers = peers + jnp.where(linked, 1, 0)

        @pl.when(linked)
        def _():
            greet((layer + c, me))

    def other_layer(way):
        return lax.rem(layer + (LAYER if way == 0 else blocks - LAYER), blocks)

    for way, end in enumerate(BETWEEN):

        @pl.when(column == end)
        def _():
            for c in COLUMNS:
                greet((other_layer(way) + c, me))

        @pl.when(relays & (column != BETWEEN[1 - way]))
        def _():
            greet((other_layer(1 - way) + end, me))

    def message(field, device, share):
        return pl.ds(pl.multiple_of((field * GRID + device) * MSG, 8), share * SLAB)

    def exchange(source, target, send_sem, recv_sem, field, peer, share):
        return pltpu.make_async_remote_copy(
            src_ref=source.at[message(field, peer, share)],
            dst_ref=target.at[message(field, me, share)],
            send_sem=send_sem.at[field, peer],
            recv_sem=recv_sem.at[field, me],
            device_id=(blk, peer),
            device_id_type=MESH,
        )

    def arrival(source, target, send_sem, recv_sem, field, peer, share):
        return pltpu.make_async_remote_copy(
            src_ref=source.at[message(field, peer, share)],
            dst_ref=target.at[message(field, peer, share)],
            send_sem=send_sem.at[field, peer],
            recv_sem=recv_sem.at[field, peer],
            device_id=(blk, peer),
            device_id_type=MESH,
        )

    def keep(source, target, field, way, share):
        here = message(field, me, share)
        return pltpu.make_async_copy(source.at[here], target.at[here], self_sem.at[way, field])

    buffers = ((sent, got, fwd_send, fwd_recv), (ret_sent, ret_got, bwd_send, bwd_recv))

    def by_parity(run):
        for parity in range(2):

            @pl.when(me % 2 == parity)
            def _():
                run(parity)

    def send_all(field, way):
        def run(parity):
            for d in (4, 3, 5, 2, 6, 1, 7):
                share = SHARE[parity if way else (parity + d) % 2]
                exchange(*buffers[way], field, lax.rem(me + d, GRID), share).start()
            keep(*buffers[way][:2], field, way, SHARE[parity]).start()

        by_parity(run)

    def await_all(field, way):
        def run(parity):
            keep(*buffers[way][:2], field, way, SHARE[parity]).wait()
            for d in range(1, GRID):
                share = SHARE[(parity + d) % 2 if way else parity]
                arrival(*buffers[way], field, lax.rem(me + d, GRID), share).wait_recv()

        by_parity(run)

    def await_sent(field, way):
        def run(parity):
            for d in range(1, GRID):
                share = SHARE[parity if way else (parity + d) % 2]
                exchange(*buffers[way], field, lax.rem(me + d, GRID), share).wait_send()

        by_parity(run)

    def band_rows(band):
        return pl.ds(pl.multiple_of(band * (SLAB * ROWS), 8), SLAB * ROWS)

    travel = ((band_out, band_in), (theirs_out, theirs_in))
    planes = SLAB // len(COLUMNS)

    def piece_rows(band, index):
        return pl.ds(pl.multiple_of((band * SLAB + index * planes) * ROWS, 8), planes * ROWS)

    def stop_rows(way, band):
        return pl.ds((way * 2 + band) * planes * ROWS, planes * ROWS)

    def to_block(way, band):
        source, target = travel[way]
        return pltpu.make_async_remote_copy(
            src_ref=source.at[band_rows(band)],
            dst_ref=target.at[band_rows(band)],
            send_sem=blk_send.at[way, band],
            recv_sem=blk_recv.at[way, band],
            device_id=((after, before)[way], me),
            device_id_type=MESH,
        )

    def to_column(way, band, index):
        if COLUMNS[index] == BETWEEN[way]:
            target = travel[way][1].at[piece_rows(band, index)]
            done = last_recv.at[way, band, index]
            place = other_layer(way) + BETWEEN[1 - way]
        else:
            target, done = stop.at[stop_rows(way, band)], stop_recv.at[way, band]
            place = layer + COLUMNS[index]
        return pltpu.make_async_remote_copy(
            src_ref=travel[way][0].at[piece_rows(band, index)],
            dst_ref=target,
            send_sem=first_send.at[way, band, index],
            recv_sem=done,
            device_id=(place, me),
            device_id_type=MESH,
        )

    def from_column(way, band, index):
        return pltpu.make_async_remote_copy(
            src_ref=stop.at[stop_rows(way, band)],
            dst_ref=travel[way][1].at[piece_rows(band, index)],
            send_sem=second_send.at[way, band],
            recv_sem=last_recv.at[way, band, index],
            device_id=(other_layer(way) + BETWEEN[1 - way], me),
            device_id_type=MESH,
        )

    def depart(way, band):
        start = BETWEEN[way]

        @pl.when(column != start)
        def _():
            to_block(way, band).start()

        @pl.when(column == start)
        def _():
            for index in range(len(COLUMNS)):
                to_column(way, band, index).start()

    def relay_in(way, band):
        @pl.when(relays & (column != BETWEEN[way]))
        def _():
            to_column(way, band, COLUMNS.index(BETWEEN[1 - way])).wait_recv()
            from_column(way, band, piece).start()

    def arrive(way, band):
        end = BETWEEN[1 - way]

        @pl.when(column != end)
        def _():
            to_block(way, band).wait_recv()

        @pl.when(column == end)
        def _():
            for index in range(len(COLUMNS)):
                from_column(way, band, index).wait_recv()

    def departed(way, band):
        start = BETWEEN[way]

        @pl.when(column != start)
        def _():
            to_block(way, band).wait_send()

        @pl.when(column == start)
        def _():
            for index in range(len(COLUMNS)):
                to_column(way, band, index).wait_send()

        @pl.when(relays & (column != start))
        def _():
            from_column(way, band, 0).wait_send()

    def put_packed(ref, band, x, plane):
        start = pl.multiple_of((band * SLAB + x) * ROWS, 8)
        for k, part in enumerate(pack(plane)):
            ref[pl.ds(start + 24 * k, 24), :] = part

    def get_packed(ref, band, x):
        start = pl.multiple_of((band * SLAB + x) * ROWS, 8)
        return unpack([ref[pl.ds(start + 24 * k, 24), :] for k in range(3)])

    for band in range(2):

        @pl.loop(0, SLAB)
        def _(x):
            plane = own_ref[band, x]
            bands[band, x] = plane
            put_packed(band_out, band, x, plane)

    pl.semaphore_wait(barrier, peers)
    for band in range(2):
        depart(0, band)

    acc[...] = jnp.zeros_like(acc)

    def pair(field):
        first = jnp.where(field < 3, field // 2, (field + 1) % 2)
        second = jnp.where(field < 3, (field + 1) // 2, 2 + (field - 3) // 2)
        return first, second

    def forward(field):
        first, second = pair(field)
        for group in range(0, SLAB, 4):
            density = bands[first, pl.ds(group, 4)] * bands[second, pl.ds(group, 4)]
            along_z = from_right(density.reshape(4 * NG, NG), right_ref)
            for i in range(4):
                plane = from_left(plane_ref[...], along_z[i * NG : (i + 1) * NG])
                parts = pack(plane)
                base = field * (GRID * MSG) + group + i
                for t in range(8):
                    tile = parts[t // 3][t % 3 * 8 : t % 3 * 8 + 8]
                    sent[pl.ds(base + t * SLAB, GRID, stride=MSG), :] = tile
                for t in (8, 9):
                    tile = parts[2][4 * t - 16 : 4 * t - 12]
                    sent[pl.ds(base + MSG + t * SLAB, GRID // 2, stride=2 * MSG), :] = tile

    def make_coulomb():
        factor = 4.0 * np.pi / (2.0 * np.pi / BOX_EDGE) ** 2 / float(NG) ** 3

        def square(index):
            folded = jnp.minimum(index, NG - index)
            return folded * folded

        kx = lax.broadcasted_iota(jnp.int32, (NG, 128), 0)
        lane = lax.broadcasted_iota(jnp.int32, (NG, 128), 1)

        @pl.loop(0, SHARE[1])
        def _(t):
            row = jnp.where(t < 8, t * GRID + me, 32 + 4 * t + me // 2)
            part, a = row // 24, row % 24
            ky = jnp.where(lane < NG, 24 * part + a, 72 + a)
            kz = jnp.where(lane < NG, lane, 32 * part + lane - NG)
            total = square(kx) + square(ky) + square(kz)
            safe = jnp.maximum(total, 1).astype(F32)
            coulomb[t] = jnp.where(total > 0, factor / safe, 0.0)

    def solve(field):
        await_all(field, 0)
        base = field * (GRID * MSG)

        def solve_tile(t):
            rows = jnp.concatenate(
                [got[pl.ds(base + t * SLAB + x, GRID, stride=MSG), :] for x in range(SLAB)],
                axis=0,
            )
            spectrum = from_left(there_ref[...], rows) * coulomb[t]
            mixed = from_left(back_ref[...], spectrum)
            for x in range(SLAB):
                ret_sent[pl.ds(base + t * SLAB + x, GRID, stride=MSG), :] = mixed[
                    x * GRID : (x + 1) * GRID
                ]

        for t in range(SHARE[0]):
            solve_tile(t)

        @pl.when(me % 2 == 1)
        def _():
            for t in range(SHARE[0], SHARE[1]):
                solve_tile(t)

        send_all(field, 1)

    def backward(field):
        await_all(field, 1)
        first, second = pair(field)
        base = field * (GRID * MSG)
        for group in range(0, SLAB, 4):
            planes = []
            for i in range(4):
                tiles = [
                    ret_got[pl.ds(base + t * SLAB + group + i, GRID, stride=MSG), :]
                    for t in range(8)
                ]
                start = base + MSG + group + i
                halves = [
                    ret_got[pl.ds(start + t * SLAB, GRID // 2, stride=2 * MSG), :]
                    for t in (8, 9)
                ]
                tiles.append(jnp.concatenate(halves, axis=0))
                parts = [jnp.concatenate(tiles[3 * k : 3 * k + 3], axis=0) for k in range(3)]
                planes.append(from_left(plane_ref[...], unpack(parts)))
            potential = from_right(jnp.concatenate(planes, axis=0), right_ref)
            potential = potential.reshape(4, NG, NG)
            here = pl.ds(group, 4)
            acc[first, here] += potential * bands[second, here]

            @pl.when(first != second)
            def _():
                acc[second, here] += potential * bands[first, here]

    def give_back(band):
        @pl.loop(0, SLAB)
        def _(x):
            put_packed(theirs_out, band, x, acc[2 + band, x])

        depart(1, band)

    def at(step, fields):
        return sum(jnp.where(step == i, field, 0) for i, field in enumerate(fields))

    @pl.loop(0, len(FORWARD))
    def _(step):
        @pl.when(step == 3)
        def _():
            for band in range(2):
                arrive(0, band)

                @pl.loop(0, SLAB)
                def _(x):
                    bands[2 + band, x] = get_packed(band_in, band, x)

        forward_field = at(step, FORWARD)

        @pl.when(forward_field >= 0)
        def _():
            forward(forward_field)

        @pl.when(step == 1)
        def _():
            for band in range(2):
                relay_in(0, band)

        @pl.when(forward_field >= 0)
        def _():
            send_all(forward_field, 0)

        @pl.when(step == 2)
        def _():
            make_coulomb()

        solve_field = at(step, SOLVE)
        backward_field = at(step, BACKWARD)

        @pl.when((solve_field >= 0) & (step < 12))
        def _():
            solve(solve_field)

        @pl.when(backward_field >= 0)
        def _():
            backward(backward_field)

        @pl.when(step == 10)
        def _():
            give_back(0)

        @pl.when(step == 12)
        def _():
            give_back(1)
            relay_in(1, 0)

        @pl.when(step == 13)
        def _():
            relay_in(1, 1)

        @pl.when((solve_field >= 0) & (step >= 12))
        def _():
            solve(solve_field)

    for band in range(2):
        arrive(1, band)

        @pl.loop(0, SLAB)
        def _(x):
            out_ref[band, x] = -(acc[band, x] + get_packed(theirs_in, band, x))

    @pl.loop(0, FIELDS)
    def _(field):
        for way in range(2):
            await_sent(field, way)

    for band in range(2):
        for way in range(2):
            departed(way, band)


def body(blocks, bands):
    count, slab, plane = bands.shape
    own = bands.reshape(count, slab, NG, NG)
    constants = [jnp.asarray(table) for table in tables()]
    vmem = pl.BlockSpec(memory_space=pltpu.VMEM)
    messages = pltpu.VMEM((FIELDS * GRID * MSG, 128), F32)
    packed = pltpu.VMEM((count * SLAB * ROWS, 128), F32)
    stops = pltpu.VMEM((2 * count * (SLAB // len(COLUMNS)) * ROWS, 128), F32)
    out = pl.pallas_call(
        functools.partial(kernel, blocks),
        out_shape=jax.ShapeDtypeStruct((count, slab, NG, NG), F32),
        in_specs=[vmem] * 5,
        out_specs=vmem,
        scratch_shapes=[
            pltpu.VMEM((2 * count, SLAB, NG, NG), F32),
            pltpu.VMEM((2 * count, SLAB, NG, NG), F32),
            pltpu.VMEM((SHARE[1], NG, 128), F32),
            messages,
            messages,
            messages,
            messages,
            packed,
            packed,
            packed,
            packed,
            pltpu.SemaphoreType.DMA((FIELDS, GRID)),
            pltpu.SemaphoreType.DMA((FIELDS, GRID)),
            pltpu.SemaphoreType.DMA((FIELDS, GRID)),
            pltpu.SemaphoreType.DMA((FIELDS, GRID)),
            pltpu.SemaphoreType.DMA((2, FIELDS)),
            pltpu.SemaphoreType.DMA((2, 2)),
            pltpu.SemaphoreType.DMA((2, 2)),
            stops,
            pltpu.SemaphoreType.DMA((2, 2, len(COLUMNS))),
            pltpu.SemaphoreType.DMA((2, 2)),
            pltpu.SemaphoreType.DMA((2, 2)),
            pltpu.SemaphoreType.DMA((2, 2, len(COLUMNS))),
        ],
        compiler_params=pltpu.CompilerParams(
            collective_id=0, has_side_effects=True, vmem_limit_bytes=48 * 1024 * 1024
        ),
    )(own, *constants)
    return out.reshape(count, slab, plane)


def solution(mesh):
    spec = P("blk", "grid", None)
    return jax.shard_map(
        functools.partial(body, mesh.shape["blk"]),
        mesh=mesh,
        in_specs=(spec,),
        out_specs=spec,
        check_vma=False,
    )
```

profile of v0, /device:TPU:1, one launch (start us, length us, event | category | flops | bytes accessed | tf_op | source)
XLA Modules:
  0.0 179.4 jit_solution(9092223428921965715)
XLA Ops:
  0.0 2.0 %reshape.6 = f32[2,12,96,96]{3,2,0,1:T(8,128)S(1)} reshape(f32[2,12,9216]{2,0,1:T(2,128)} %param.5) | data formatting | bytes 1769472 | tf_op jit(solution)/shard_map/reshape | solution.py:545
  2.0 0.0 copy-start
  2.0 0.0 copy-start.1
  2.0 0.0 copy-start.2
  2.0 0.0 copy-start.3
  2.0 0.1 copy.8.own_ref
  2.1 0.8 copy-done
  2.9 0.1 copy-done.1
  3.0 0.1 copy-done.2
  3.1 0.1 copy-done.3
  3.1 174.0 %shard_map.55 = f32[2,12,96,96]{3,2,1,0:T(8,128)S(1)} custom-call(f32[2,12,96,96]{3,2,1,0:T(8,128)S(1)} %copy.8.own_ref, bf16[96,384]{1,0:T(8,128)(2,1)S(1)} %copy-done.3, bf16[288,192]{1,0:T(8,128)(2,1)S(1)} %copy-done.2, bf16[288,192]{1,0:T(8,128)(2,1)S(1)} %copy-done.1, bf16[288,192]{1,0:T(8,128)(2,1)S(1)} %copy-done), custom_call_target="tpu_custom_call" | custom-call | tf_op jit(solution)/shard_map/pallas_call | solution.py:551
  177.1 0.7 reshape.8
  177.8 1.6 copy.10
Async XLA Ops:
  2.0 0.9 copy-start
  2.0 1.0 copy-start.1
  2.0 1.0 copy-start.2
  2.0 1.1 copy-start.3
where the time goes:
time: 180 us; the launch traced here: 179 us
  Pallas kernels  174 us (97%)
  local copies, waits for them, and re-layouts  5.35 us (3%)
    pallas_call x1, Pallas kernels, body(): pl.pallas_call(functools.partial(kernel, blocks), out_shape=jax.ShapeDtyp...  174 us

commit v1 on v0

--- a/solution.py
+++ b/solution.py
@@ -354,8 +354,8 @@
             bands[band, x] = plane
             put_packed(band_out, band, x, plane)
 
-    pl.semaphore_wait(barrier, peers)
-    for band in range(2):
+        if band == 0:
+            pl.semaphore_wait(barrier, peers)
         depart(0, band)
 
     acc[...] = jnp.zeros_like(acc)
@@ -467,9 +467,10 @@
 
     @pl.loop(0, len(FORWARD))
     def _(step):
-        @pl.when(step == 3)
-        def _():
-            for band in range(2):
+        for band in range(2):
+
+            @pl.when(step == 3 + 2 * band)
+            def _():
                 arrive(0, band)
 
                 @pl.loop(0, SLAB)
@@ -482,9 +483,10 @@
         def _():
             forward(forward_field)
 
-        @pl.when(step == 1)
-        def _():
-            for band in range(2):
+        for band in range(2):
+
+            @pl.when(step == band)
+            def _():
                 relay_in(0, band)
 
         @pl.when(forward_field >= 0)
@@ -498,10 +500,16 @@
         solve_field = at(step, SOLVE)
         backward_field = at(step, BACKWARD)
 
-        @pl.when((solve_field >= 0) & (step < 12))
+        solve_late = (step == 10) | (step >= 12)
+
+        @pl.when((solve_field >= 0) & ~solve_late)
         def _():
             solve(solve_field)
 
+        @pl.when(step == 12)
+        def _():
+            relay_in(1, 0)
+
         @pl.when(backward_field >= 0)
         def _():
             backward(backward_field)
@@ -513,13 +521,12 @@
         @pl.when(step == 12)
         def _():
             give_back(1)
-            relay_in(1, 0)
 
         @pl.when(step == 13)
         def _():
             relay_in(1, 1)
 
-        @pl.when((solve_field >= 0) & (step >= 12))
+        @pl.when((solve_field >= 0) & solve_late)
         def _():
             solve(solve_field)
 

time: 180 us -> 183 us (1.017)
  the two profiles are of different devices: /device:TPU:1 before, /device:TPU:2 now
where the time goes in v1:
time: 183 us
  Pallas kernels  178 us (97%)
  local copies, waits for them, and re-layouts  5.35 us (3%)
    pallas_call x1, Pallas kernels, body(): pl.pallas_call(functools.partial(kernel, blocks), out_shape=jax.ShapeDtyp...  178 us

profile of v1, /device:TPU:2, one launch (start us, length us, event | category | flops | bytes accessed | tf_op | source)
XLA Modules:
  0.0 183.2 jit_solution(4680169913243705144)
XLA Ops:
  0.0 2.0 %reshape.6 = f32[2,12,96,96]{3,2,0,1:T(8,128)S(1)} reshape(f32[2,12,9216]{2,0,1:T(2,128)} %param.5) | data formatting | bytes 1769472 | tf_op jit(solution)/shard_map/reshape | solution.py:552
  2.0 0.0 copy-start
  2.0 0.0 copy-start.1
  2.0 0.0 copy-start.2
  2.0 0.0 copy-start.3
  2.0 0.1 copy.8.own_ref
  2.1 0.8 copy-done
  2.9 0.1 copy-done.1
  3.0 0.1 copy-done.2
  3.1 0.1 copy-done.3
  3.1 177.8 %shard_map.55 = f32[2,12,96,96]{3,2,1,0:T(8,128)S(1)} custom-call(f32[2,12,96,96]{3,2,1,0:T(8,128)S(1)} %copy.8.own_ref, bf16[96,384]{1,0:T(8,128)(2,1)S(1)} %copy-done.3, bf16[288,192]{1,0:T(8,128)(2,1)S(1)} %copy-done.2, bf16[288,192]{1,0:T(8,128)(2,1)S(1)} %copy-done.1, bf16[288,192]{1,0:T(8,128)(2,1)S(1)} %copy-done), custom_call_target="tpu_custom_call" | custom-call | tf_op jit(solution)/shard_map/pallas_call | solution.py:558
  181.0 0.7 reshape.8
  181.7 1.6 copy.10
Async XLA Ops:
  2.0 0.9 copy-start
  2.0 1.0 copy-start.1
  2.0 1.0 copy-start.2
  2.0 1.1 copy-start.3

commit v2 on v1

--- a/solution.py
+++ b/solution.py
@@ -28,6 +28,7 @@
 
 FORWARD = (0, 1, 2, 3, 4, 5, 6, -1, -1, -1, -1, -1, -1, -1, -1, -1)
 SOLVE = (-1, -1, -1, -1, -1, -1, -1, 3, 4, 5, 6, 0, 1, 2, -1, -1)
+SOLVE_FIRST = (-1, -1, -1, -1, -1, -1, -1, 3, 4, 5, 6, -1, 0, 1, 2, -1)
 BACKWARD = (-1, -1, -1, -1, -1, -1, -1, -1, -1, 3, 4, 5, 6, 0, 1, 2)
 
 
@@ -483,52 +484,49 @@
         def _():
             forward(forward_field)
 
+        @pl.when(step == 1)
+        def _():
+            for band in range(2):
+                relay_in(0, band)
+
+        @pl.when(forward_field >= 0)
+        def _():
+            send_all(forward_field, 0)
+
+        @pl.when(step == 2)
+        def _():
+            make_coulomb()
+
+        solve_field = jnp.where(column == 0, at(step, SOLVE_FIRST), at(step, SOLVE))
+        backward_field = at(step, BACKWARD)
+
+        solve_late = (step == 10) | (step == 12) | ((step == 13) & (column != 0))
+
+        @pl.when((solve_field >= 0) & ~solve_late)
+        def _():
+            solve(solve_field)
+
+        @pl.when(backward_field >= 0)
+        def _():
+            backward(backward_field)
+
+        @pl.when(step == 10)
+        def _():
+            give_back(0)
+
+        @pl.when(step == 12)
+        def _():
+            give_back(1)
+
+        @pl.when((solve_field >= 0) & solve_late)
+        def _():
+            solve(solve_field)
+
         for band in range(2):
 
-            @pl.when(step == band)
+            @pl.when(step == 12 + 2 * band)
             def _():
-                relay_in(0, band)
-
-        @pl.when(forward_field >= 0)
-        def _():
-            send_all(forward_field, 0)
-
-        @pl.when(step == 2)
-        def _():
-            make_coulomb()
-
-        solve_field = at(step, SOLVE)
-        backward_field = at(step, BACKWARD)
-
-        solve_late = (step == 10) | (step >= 12)
-
-        @pl.when((solve_field >= 0) & ~solve_late)
-        def _():
-            solve(solve_field)
-
-        @pl.when(step == 12)
-        def _():
-            relay_in(1, 0)
-
-        @pl.when(backward_field >= 0)
-        def _():
-            backward(backward_field)
-
-        @pl.when(step == 10)
-        def _():
-            give_back(0)
-
-        @pl.when(step == 12)
-        def _():
-            give_back(1)
-
-        @pl.when(step == 13)
-        def _():
-            relay_in(1, 1)
-
-        @pl.when((solve_field >= 0) & solve_late)
-        def _():
-            solve(solve_field)
+                relay_in(1, band)
 
     for band in range(2):
         arrive(1, band)

time: 183 us -> 185 us (1.011)
  the two profiles are of different devices: /device:TPU:2 before, /device:TPU:35 now
where the time goes in v2:
time: 185 us; the launch traced here: 184 us
  Pallas kernels  179 us (97%)
  local copies, waits for them, and re-layouts  5.35 us (3%)
    pallas_call x1, Pallas kernels, body(): pl.pallas_call(functools.partial(kernel, blocks), out_shape=jax.ShapeDtyp...  179 us

profile of v2, /device:TPU:35, one launch (start us, length us, event | category | flops | bytes accessed | tf_op | source)
XLA Modules:
  0.0 184.4 jit_solution(1720093794364599410)
XLA Ops:
  0.0 2.0 %reshape.6 = f32[2,12,96,96]{3,2,0,1:T(8,128)S(1)} reshape(f32[2,12,9216]{2,0,1:T(2,128)} %param.5) | data formatting | bytes 1769472 | tf_op jit(solution)/shard_map/reshape | solution.py:550
  2.0 0.0 copy-start
  2.0 0.0 copy-start.1
  2.0 0.0 copy-start.2
  2.0 0.0 copy-start.3
  2.0 0.1 copy.8.own_ref
  2.1 0.8 copy-done
  2.9 0.1 copy-done.1
  3.0 0.1 copy-done.2
  3.1 0.1 copy-done.3
  3.1 179.0 %shard_map.55 = f32[2,12,96,96]{3,2,1,0:T(8,128)S(1)} custom-call(f32[2,12,96,96]{3,2,1,0:T(8,128)S(1)} %copy.8.own_ref, bf16[96,384]{1,0:T(8,128)(2,1)S(1)} %copy-done.3, bf16[288,192]{1,0:T(8,128)(2,1)S(1)} %copy-done.2, bf16[288,192]{1,0:T(8,128)(2,1)S(1)} %copy-done.1, bf16[288,192]{1,0:T(8,128)(2,1)S(1)} %copy-done), custom_call_target="tpu_custom_call" | custom-call | tf_op jit(solution)/shard_map/pallas_call | solution.py:556
  182.1 0.7 reshape.8
  182.8 1.6 copy.10
Async XLA Ops:
  2.0 0.9 copy-start
  2.0 1.0 copy-start.1
  2.0 1.0 copy-start.2
  2.0 1.1 copy-start.3

commit v3 on v0

--- a/solution.py
+++ b/solution.py
@@ -23,7 +23,9 @@
 FIELDS = 7
 
 LAYER = 16
-COLUMNS = (0, 1, 2, 3, 4, 7, 8, 11, 12, 13, 14, 15)
+COLUMNS = (0, 1, 2, 3, 4, 7, 8, 11, 12, 13, 14, 15, 5, 6, 9, 10)
+LARGE = 12
+PIECE = 56, 48
 BETWEEN = LAYER - 1, 0
 
 FORWARD = (0, 1, 2, 3, 4, 5, 6, -1, -1, -1, -1, -1, -1, -1, -1, -1)
@@ -245,13 +247,18 @@
         return pl.ds(pl.multiple_of(band * (SLAB * ROWS), 8), SLAB * ROWS)
 
     travel = ((band_out, band_in), (theirs_out, theirs_in))
-    planes = SLAB // len(COLUMNS)
-
-    def piece_rows(band, index):
-        return pl.ds(pl.multiple_of((band * SLAB + index * planes) * ROWS, 8), planes * ROWS)
-
-    def stop_rows(way, band):
-        return pl.ds((way * 2 + band) * planes * ROWS, planes * ROWS)
+
+    def piece_rows(band, index, size):
+        start = index * PIECE[0]
+        if size == PIECE[1]:
+            start = LARGE * PIECE[0] + (index - LARGE) * PIECE[1]
+        return pl.ds(pl.multiple_of(band * (SLAB * ROWS) + start, 8), size)
+
+    def stop_rows(way, band, size):
+        return pl.ds((way * 2 + band) * PIECE[0], size)
+
+    def size_of(index):
+        return PIECE[0] if index < LARGE else PIECE[1]
 
     def to_block(way, band):
         source, target = travel[way]
@@ -266,14 +273,14 @@
 
     def to_column(way, band, index):
         if COLUMNS[index] == BETWEEN[way]:
-            target = travel[way][1].at[piece_rows(band, index)]
+            target = travel[way][1].at[piece_rows(band, index, size_of(index))]
             done = last_recv.at[way, band, index]
             place = other_layer(way) + BETWEEN[1 - way]
         else:
-            target, done = stop.at[stop_rows(way, band)], stop_recv.at[way, band]
+            target, done = stop.at[stop_rows(way, band, size_of(index))], stop_recv.at[way, band]
             place = layer + COLUMNS[index]
         return pltpu.make_async_remote_copy(
-            src_ref=travel[way][0].at[piece_rows(band, index)],
+            src_ref=travel[way][0].at[piece_rows(band, index, size_of(index))],
             dst_ref=target,
             send_sem=first_send.at[way, band, index],
             recv_sem=done,
@@ -281,10 +288,10 @@
             device_id_type=MESH,
         )
 
-    def from_column(way, band, index):
+    def from_column(way, band, index, size):
         return pltpu.make_async_remote_copy(
-            src_ref=stop.at[stop_rows(way, band)],
-            dst_ref=travel[way][1].at[piece_rows(band, index)],
+            src_ref=stop.at[stop_rows(way, band, size)],
+            dst_ref=travel[way][1].at[piece_rows(band, index, size)],
             send_sem=second_send.at[way, band],
             recv_sem=last_recv.at[way, band, index],
             device_id=(other_layer(way) + BETWEEN[1 - way], me),
@@ -306,8 +313,12 @@
     def relay_in(way, band):
         @pl.when(relays & (column != BETWEEN[way]))
         def _():
-            to_column(way, band, COLUMNS.index(BETWEEN[1 - way])).wait_recv()
-            from_column(way, band, piece).start()
+            for index, large in ((COLUMNS.index(BETWEEN[1 - way]), True), (LARGE, False)):
+
+                @pl.when((piece < LARGE) == large)
+                def _():
+                    to_column(way, band, index).wait_recv()
+                    from_column(way, band, piece, size_of(index)).start()
 
     def arrive(way, band):
         end = BETWEEN[1 - way]
@@ -319,7 +330,7 @@
         @pl.when(column == end)
         def _():
             for index in range(len(COLUMNS)):
-                from_column(way, band, index).wait_recv()
+                from_column(way, band, index, size_of(index)).wait_recv()
 
     def departed(way, band):
         start = BETWEEN[way]
@@ -335,7 +346,11 @@
 
         @pl.when(relays & (column != start))
         def _():
-            from_column(way, band, 0).wait_send()
+            for size, large in zip(PIECE, (True, False)):
+
+                @pl.when((piece < LARGE) == large)
+                def _():
+                    from_column(way, band, piece, size).wait_send()
 
     def put_packed(ref, band, x, plane):
         start = pl.multiple_of((band * SLAB + x) * ROWS, 8)
@@ -547,7 +562,7 @@
     vmem = pl.BlockSpec(memory_space=pltpu.VMEM)
     messages = pltpu.VMEM((FIELDS * GRID * MSG, 128), F32)
     packed = pltpu.VMEM((count * SLAB * ROWS, 128), F32)
-    stops = pltpu.VMEM((2 * count * (SLAB // len(COLUMNS)) * ROWS, 128), F32)
+    stops = pltpu.VMEM((2 * count * PIECE[0], 128), F32)
     out = pl.pallas_call(
         functools.partial(kernel, blocks),
         out_shape=jax.ShapeDtypeStruct((count, slab, NG, NG), F32),

time: 180 us -> 175 us (0.972)
  Pallas kernels: 174 us -> 169 us
    pallas_call x1, Pallas kernels: 174 us -> 169 us  [body(): pl.pallas_call(functools.partial(kernel, blocks), out_shape=jax.ShapeDtyp...]
where the time goes in v3:
time: 175 us
  Pallas kernels  169 us (97%)
  local copies, waits for them, and re-layouts  5.35 us (3%)
    pallas_call x1, Pallas kernels, body(): pl.pallas_call(functools.partial(kernel, blocks), out_shape=jax.ShapeDtyp...  169 us

profile of v3, /device:TPU:1, one launch (start us, length us, event | category | flops | bytes accessed | tf_op | source)
XLA Modules:
  0.0 174.5 jit_solution(5292282090694420206)
XLA Ops:
  0.0 2.0 %reshape.6 = f32[2,12,96,96]{3,2,0,1:T(8,128)S(1)} reshape(f32[2,12,9216]{2,0,1:T(2,128)} %param.5) | data formatting | bytes 1769472 | tf_op jit(solution)/shard_map/reshape | solution.py:560
  2.0 0.0 copy-start
  2.0 0.0 copy-start.1
  2.0 0.0 copy-start.2
  2.0 0.0 copy-start.3
  2.0 0.1 copy.8.own_ref
  2.1 0.8 copy-done
  2.9 0.1 copy-done.1
  3.0 0.1 copy-done.2
  3.1 0.1 copy-done.3
  3.1 169.1 %shard_map.55 = f32[2,12,96,96]{3,2,1,0:T(8,128)S(1)} custom-call(f32[2,12,96,96]{3,2,1,0:T(8,128)S(1)} %copy.8.own_ref, bf16[96,384]{1,0:T(8,128)(2,1)S(1)} %copy-done.3, bf16[288,192]{1,0:T(8,128)(2,1)S(1)} %copy-done.2, bf16[288,192]{1,0:T(8,128)(2,1)S(1)} %copy-done.1, bf16[288,192]{1,0:T(8,128)(2,1)S(1)} %copy-done), custom_call_target="tpu_custom_call" | custom-call | tf_op jit(solution)/shard_map/pallas_call | solution.py:566
  172.2 0.7 reshape.8
  172.9 1.6 copy.10
Async XLA Ops:
  2.0 0.9 copy-start
  2.0 1.0 copy-start.1
  2.0 1.0 copy-start.2
  2.0 1.1 copy-start.3

commit v4 on v3

--- a/solution.py
+++ b/solution.py
@@ -482,9 +482,10 @@
 
     @pl.loop(0, len(FORWARD))
     def _(step):
-        @pl.when(step == 3)
-        def _():
-            for band in range(2):
+        for band in range(2):
+
+            @pl.when(step == 3 + 2 * band)
+            def _():
                 arrive(0, band)
 
                 @pl.loop(0, SLAB)
@@ -530,13 +531,13 @@
             give_back(1)
             relay_in(1, 0)
 
+        @pl.when((solve_field >= 0) & (step >= 12))
+        def _():
+            solve(solve_field)
+
         @pl.when(step == 13)
         def _():
             relay_in(1, 1)
-
-        @pl.when((solve_field >= 0) & (step >= 12))
-        def _():
-            solve(solve_field)
 
     for band in range(2):
         arrive(1, band)

time: 175 us -> 175 us (level)
  no operation moved by 1% of the time
where the time goes in v4:
time: 175 us
  Pallas kernels  169 us (97%)
  local copies, waits for them, and re-layouts  5.35 us (3%)
    pallas_call x1, Pallas kernels, body(): pl.pallas_call(functools.partial(kernel, blocks), out_shape=jax.ShapeDtyp...  169 us

profile of v4, /device:TPU:1, one launch (start us, length us, event | category | flops | bytes accessed | tf_op | source)
XLA Modules:
  0.0 174.5 jit_solution(17146604593653445696)
XLA Ops:
  0.0 2.0 %reshape.6 = f32[2,12,96,96]{3,2,0,1:T(8,128)S(1)} reshape(f32[2,12,9216]{2,0,1:T(2,128)} %param.5) | data formatting | bytes 1769472 | tf_op jit(solution)/shard_map/reshape | solution.py:561
  2.0 0.0 copy-start
  2.0 0.0 copy-start.1
  2.0 0.0 copy-start.2
  2.0 0.0 copy-start.3
  2.0 0.1 copy.8.own_ref
  2.1 0.8 copy-done
  2.9 0.1 copy-done.1
  3.0 0.1 copy-done.2
  3.1 0.1 copy-done.3
  3.1 169.1 %shard_map.55 = f32[2,12,96,96]{3,2,1,0:T(8,128)S(1)} custom-call(f32[2,12,96,96]{3,2,1,0:T(8,128)S(1)} %copy.8.own_ref, bf16[96,384]{1,0:T(8,128)(2,1)S(1)} %copy-done.3, bf16[288,192]{1,0:T(8,128)(2,1)S(1)} %copy-done.2, bf16[288,192]{1,0:T(8,128)(2,1)S(1)} %copy-done.1, bf16[288,192]{1,0:T(8,128)(2,1)S(1)} %copy-done), custom_call_target="tpu_custom_call" | custom-call | tf_op jit(solution)/shard_map/pallas_call | solution.py:567
  172.2 0.7 reshape.8
  172.9 1.6 copy.10
Async XLA Ops:
  2.0 0.9 copy-start
  2.0 1.0 copy-start.1
  2.0 1.0 copy-start.2
  2.0 1.1 copy-start.3
